TPU v7x, 768 devices: a whole 4x8x12 slice. The times are simulated.
768 devices in a mesh: src: 96 (over y_hi, z, core), tgt: 8 (over x, y_lo).
Axes of the slice: x: 4, y: 8 (y_hi: 4, y_lo: 2; y = y_hi * 2 + y_lo), z: 12, core: 2. Of those that a mesh axis runs over, the one named last changes fastest.
Arguments:
- source_items: bfloat16 [49152, 128], P('src'), may hold values from -4 to 4
- target_items: bfloat16 [32768, 128], P('tgt'), may hold values from -4 to 4
- source_mass: float32 [49152], P('src'), may hold values from 0.3 to 4.5
- target_mass: float32 [32768], P('tgt'), may hold values from 0.5 to 2
Outputs:
- mapped: float32 [49152, 128], P('src', 'tgt')
- potential: float32 [32768], P('tgt')
All inputs are finite; a program needn't handle non-finite values.
Results may differ from a plain program's by a relative error of at most 0.0014.
Values sent between devices are 32-bit elements; how exact they have to be, the bound alone decides.
A program may use at most 32 MiB of HBM per device.

v0:
```python
import math

import jax
import jax.numpy as jnp
from jax import lax
from jax.sharding import PartitionSpec as P

ITERS = 3


def kernel_of(source_items, target_items):
    logits = lax.dot_general(
        source_items, target_items, (((1,), (1,)), ((), ())), preferred_element_type=jnp.float32
    )
    return jnp.exp(logits * (2.0 / math.sqrt(source_items.shape[1])))


def on_device(source_items, target_items, source_mass, target_mass):
    row_scale = jnp.ones((source_items.shape[0],), jnp.float32)
    col_scale = jnp.ones((target_items.shape[0],), jnp.float32)
    for rounds in range(ITERS):
        kernel_tile = kernel_of(source_items, target_items)
        col_part = jnp.dot(row_scale, kernel_tile, precision=lax.Precision.HIGHEST)
        fresh_row = row_scale
        if rounds + 1 < ITERS:
            row_part = jnp.dot(kernel_tile, col_scale, precision=lax.Precision.HIGHEST)
            row_total = lax.psum(row_part, "tgt")
            fresh_row = source_mass / row_total
        col_total = lax.psum(col_part, "src")
        col_scale = target_mass / col_total
        row_scale = fresh_row
    kernel_tile = kernel_of(source_items, target_items)
    weights = (kernel_tile * col_scale[None, :]).astype(jnp.bfloat16)
    numerator = jnp.dot(weights, target_items, preferred_element_type=jnp.float32)
    unit_column = jnp.ones((target_items.shape[0],), jnp.bfloat16)
    denominator = jnp.dot(weights, unit_column, preferred_element_type=jnp.float32)
    column_width = target_items.shape[1] // lax.axis_size("tgt")
    num_total, den_total = lax.psum((numerator, denominator), "tgt")
    first_col = lax.axis_index("tgt") * column_width
    mapped = lax.dynamic_slice_in_dim(num_total, first_col, column_width, 1) / den_total[:, None]
    source_count = source_items.shape[0] * lax.axis_size("src")
    potential = jnp.log(source_count * col_scale)
    return (mapped, potential)


def solution(mesh):
    in_specs = (P("src", None), P("tgt", None), P("src"), P("tgt"))
    out_specs = (P("src", "tgt"), P("tgt"))
    return jax.shard_map(
        on_device, mesh=mesh, in_specs=in_specs, out_specs=out_specs, check_vma=False
    )
```

profile of v0, /device:TPU:1, one launch (start us, length us, event | category | flops | bytes accessed | tf_op | source)
XLA Modules:
  0.0 979.8 jit_solution(16828267958305358556)
XLA Ops:
  7.2 0.0 copy-start
  7.2 0.0 copy-start.2
  7.2 0.0 all-reduce.2.cloned.1.call-start
  7.2 1.2 copy-done
  8.4 2.2 multiply_exponential_fusion
  10.6 0.0 copy-start.1
  10.6 3.2 copy-done.1
  13.8 0.0 copy-start.3
  13.8 4.0 fusion.3
  17.9 422.4 %psum.35 = f32[4096]{0:T(1024)S(1)} all-reduce(f32[4096]{0:T(1024)S(1)} %bitcast.16), channel_id=1, replica_groups=mesh['src'=96,'tgt'=8] {'src'}, use_global_device_ids=true, to_apply=%region_0.0 | all-reduce | flops 4096 | bytes 32768 | tf_op jit(solution)/shard_map/psum | solution.py:29
  440.3 0.0 copy-done.2
  440.3 9.4 fusion.7
  449.7 15.1 %psum.36 = f32[512]{0:T(512)S(1)} all-reduce(f32[512]{0:T(512)S(1)} %bitcast.19), channel_id=1, replica_groups=mesh['src'=96,'tgt'=8] {'tgt'}, use_global_device_ids=true, to_apply=%region_1.0 | all-reduce | flops 512 | bytes 4096 | tf_op jit(solution)/shard_map/psum | solution.py:27
  464.9 0.0 copy-done.3
  464.9 6.3 fusion.8
  471.2 415.6 %psum.37 = f32[4096]{0:T(1024)S(1)} all-reduce(f32[4096]{0:T(1024)S(1)} %bitcast.15), channel_id=1, replica_groups=mesh['src'=96,'tgt'=8] {'src'}, use_global_device_ids=true, to_apply=%region_2.0 | all-reduce | flops 4096 | bytes 32768 | tf_op jit(solution)/shard_map/psum | solution.py:29
  886.9 0.6 multiply_log_fusion
  887.5 5.6 fusion.1
  893.1 0.0 all-reduce.2.cloned.1.call-update
  893.1 4.6 fusion
  897.7 12.6 %psum.39 = f32[512]{0:T(512)S(1)} all-reduce(f32[512]{0:T(512)S(1)} %bitcast.18), channel_id=1, replica_groups=mesh['src'=96,'tgt'=8] {'tgt'}, use_global_device_ids=true, to_apply=%region_4.0 | all-reduce | flops 512 | bytes 4096 | tf_op jit(solution)/shard_map/psum | solution.py:38
  910.2 61.4 %all-reduce.2.cloned.1.call-done = f32[512,128]{0,1:T(8,128)} async-done(((f32[512,128]{0,1:T(8,128)}), f32[512,128]{0,1:T(8,128)}) %all-reduce.2.cloned.1.call-update) | async-done | bytes 262160 | tf_op jit(solution)/shard_map/psum | solution.py:38
  971.6 1.4 dynamic-slice_divide_fusion
  (2 shorter events, 0.0 us)
Async XLA Ops:
  7.2 1.2 copy-start
  7.2 433.1 %copy-start.2 = (f32[4096]{0:T(1024)S(1)}, f32[4096]{0:T(1024)}, u32[]{:S(2)}) copy-start(f32[4096]{0:T(1024)} %param.7) | copy-start | bytes 49156
  7.2 964.4 %all-reduce.2.cloned.1.call-start = ((), (), s32[]{:S(2)}) async-start(), calls=%async_computation | async-start | bytes 524288 | tf_op jit(solution)/shard_map/psum | solution.py:38
  10.6 3.2 copy-start.1
  13.8 451.1 %copy-start.3 = (f32[512]{0:T(512)S(1)}, f32[512]{0:T(512)}, u32[]{:S(2)}) copy-start(f32[512]{0:T(512)} %param.6) | copy-start | bytes 6148
Sparse Core Ops, SparseCore 0:
  893.2 78.3 all-reduce.1
where the time goes:
time: 984 us; the launch traced here: 980 us
  blocking collectives  866 us (88%)
  waiting for transfers between devices  61.4 us (6%)
  matrix products  32.2 us (3%)
  between operations  14.1 us (1%)
    psum x2, blocking collectives, on_device(): col_total = lax.psum(col_part, 'src')  838 us
    psum x1, waiting for transfers between devices, on_device(): num_total, den_total = lax.psum((numerator, denominator), 'tgt')  61.4 us
  transfers between devices with their start and end apart: 1, of which 1 were waited for; matrix products, arithmetic and copies ran while one was open for 0% of the time, Pallas kernels for 0%

commit v1 on v0

v1 whole, which is shorter than its diff:
```python
import functools
import math

import jax
import jax.numpy as jnp
from jax import lax
from jax.experimental import pallas as pl
from jax.experimental.pallas import tpu as pltpu
from jax.sharding import PartitionSpec as P

ROWS = 512
COLS = 4096
EMBED = 128
DEPTH = 12
PAIR = 2
TEAM = 8
PART = COLS // TEAM
TGT = 8
SLIVER = EMBED // TGT
MESH = pl.DeviceIdType.MESH
F32 = jnp.float32
BF16 = jnp.bfloat16


def kernel(
    source_count,
    s_hbm, t_hbm, rmass_hbm, cmass_hbm,
    map_ref, pot_ref,
    s_v, text, rmass, cmass, kmat,
    col_send, col_recv, z_buf, c_buf,
    row_acc, row_buf, row_wide,
    num, num_t, num_recv, den_t, den_recv,
    load_sem, team_send, team_recv, z_send, z_recv, c_send, c_recv,
    row_send, row_recv, num_send, num_rsem, den_send, den_rsem,
):
    me_s, me_t = lax.axis_index("src"), lax.axis_index("tgt")
    core = lax.rem(me_s, PAIR)
    chip = lax.div(me_s, PAIR)
    zed = lax.rem(chip, DEPTH)
    member = lax.div(chip, DEPTH) * PAIR + core

    def mate(k):
        other = lax.rem(member + k, TEAM)
        return (
            (lax.div(other, PAIR) * DEPTH + zed) * PAIR + lax.rem(other, PAIR),
            me_t,
        )

    def level(k):
        return (
            (lax.div(member, PAIR) * DEPTH + lax.rem(zed + k, DEPTH)) * PAIR + core,
            me_t,
        )

    def across(k):
        return (me_s, lax.rem(me_t + k, TGT))

    loads = [
        pltpu.make_async_copy(s_hbm, s_v, load_sem.at[0]),
        pltpu.make_async_copy(t_hbm, text.at[:, :, pl.ds(0, EMBED)], load_sem.at[1]),
        pltpu.make_async_copy(rmass_hbm, rmass, load_sem.at[2]),
        pltpu.make_async_copy(cmass_hbm, cmass, load_sem.at[3]),
    ]
    for load in loads:
        load.start()

    barrier = pltpu.get_barrier_semaphore()
    friends = (
        [mate(k) for k in range(1, TEAM)]
        + [level(k) for k in range(1, DEPTH)]
        + [across(k) for k in range(1, TGT)]
    )
    for friend in friends:
        pl.semaphore_signal(barrier, inc=1, device_id=friend, device_id_type=MESH)

    text[:, :, pl.ds(EMBED, EMBED)] = jnp.ones((TEAM, PART, EMBED), BF16)
    loads[0].wait()
    loads[1].wait()

    def remote(src, dst, send, recv, where):
        return pltpu.make_async_remote_copy(
            src_ref=src, dst_ref=dst, send_sem=send, recv_sem=recv,
            device_id=where, device_id_type=MESH,
        )

    def spread_columns(it, part_of):
        for k in range(1, TEAM + 1):
            q = lax.rem(member + k, TEAM)
            col_send[it, k - 1] = part_of(q)
            if k < TEAM:
                if it == 0 and k == 1:
                    pl.semaphore_wait(barrier, len(friends))
                remote(
                    col_send.at[it, k - 1], col_recv.at[it, k - 1],
                    team_send.at[it], team_recv.at[it], mate(k),
                ).start()
        everyone = pl.ds(0, TEAM - 1)
        team = remote(
            col_send.at[it, everyone], col_recv.at[it, everyone],
            team_send.at[it], team_recv.at[it], mate(1),
        )
        team.wait_recv()
        total = col_send[it, TEAM - 1]
        for k in range(TEAM - 1):
            total = total + col_recv[it, k]
        z_buf[it, zed] = total
        for k in range(1, DEPTH):
            remote(
                z_buf.at[it, zed], z_buf.at[it, zed],
                z_send.at[it], z_recv.at[it], level(k),
            ).start()
        team.wait_send()
        others = pl.ds(0, DEPTH - 1)
        floor = remote(
            z_buf.at[it, others], z_buf.at[it, others],
            z_send.at[it], z_recv.at[it], level(1),
        )
        if it == 0:
            loads[3].wait()
        floor.wait_recv()
        total = z_buf[it, 0]
        for k in range(1, DEPTH):
            total = total + z_buf[it, k]
        c_buf[it, member] = cmass[member] / total
        copies = [
            remote(
                c_buf.at[it, member], c_buf.at[it, member],
                c_send.at[it], c_recv.at[it, k], mate(k),
            )
            for k in range(1, TEAM)
        ]
        for copy in copies:
            copy.start()
        floor.wait_send()

        def arrival(k):
            if k:
                copies[k - 1].wait_recv()
            return lax.rem(member + TEAM - k, TEAM)

        def flush():
            remote(
                c_buf.at[it, everyone], c_buf.at[it, everyone],
                c_send.at[it], c_recv.at[it, 1], mate(1),
            ).wait_send()

        return arrival, flush

    log2e = 1.4426950408889634
    factor = 2.0 / math.sqrt(EMBED) * log2e

    def first_part(q):
        pieces = []
        for h in range(PART // 256):
            cols = pl.ds(h * 256, 256)
            logits = lax.dot_general(
                s_v[...], text[q, cols, pl.ds(0, EMBED)],
                (((1,), (1,)), ((), ())), preferred_element_type=F32,
            )
            tile = jnp.exp2(logits * factor)
            kmat[q, :, cols] = tile
            pieces.append(jnp.sum(tile, axis=0, keepdims=True))
        return jnp.concatenate(pieces, axis=1)

    arrival, flush = spread_columns(0, first_part)
    loads[2].wait()

    for k in range(TEAM):
        q = arrival(k)
        scale = c_buf[0, q]
        fold = None
        for lane in range(PART // 128):
            cols = pl.ds(lane * 128, 128)
            term = kmat[q, :, cols] * scale[:, lane * 128 : lane * 128 + 128]
            fold = term if fold is None else fold + term
        if k == 0:
            row_acc[...] = fold
        else:
            row_acc[...] += fold
    row_buf[me_t] = jnp.sum(row_acc[...].T, axis=0, keepdims=True)
    for k in range(1, TGT):
        remote(
            row_buf.at[me_t], row_buf.at[me_t], row_send, row_recv, across(k)
        ).start()
    flush()
    rest = pl.ds(0, TGT - 1)
    rows = remote(row_buf.at[rest], row_buf.at[rest], row_send, row_recv, across(1))
    rows.wait_recv()
    total = row_buf[0]
    for k in range(1, TGT):
        total = total + row_buf[k]
    row_wide[...] = jnp.broadcast_to(rmass[...] / total, (128, ROWS)).T

    def second_part(q):
        pieces = []
        for lane in range(PART // 128):
            cols = pl.ds(lane * 128, 128)
            pieces.append(
                jnp.sum(kmat[q, :, cols] * row_wide[...], axis=0, keepdims=True)
            )
        return jnp.concatenate(pieces, axis=1)

    arrival, flush = spread_columns(1, second_part)
    rows.wait_send()

    half = ROWS // 2
    for k in range(TEAM):
        q = arrival(k)
        scale = c_buf[1, q]
        if k < TEAM - 1:
            weights = (kmat[q] * scale).astype(BF16)
            term = jnp.dot(weights, text[q], preferred_element_type=F32)
            if k == 0:
                num[...] = term
            else:
                num[...] += term
            continue
        for h in range(2):
            span = pl.ds(h * half, half)
            weights = (kmat[q, span, :] * scale).astype(BF16)
            term = jnp.dot(weights, text[q], preferred_element_type=F32)
            term = term + num[span, :]
            num_t[:, :, span] = term[:, :EMBED].T.reshape(TGT, SLIVER, half)
            den_t[:, span] = term[:, EMBED:].T[:1]
            for j in range(1, TGT):
                there = lax.rem(me_t + j, TGT)
                remote(
                    num_t.at[there, :, span], num_recv.at[j - 1, :, span],
                    num_send.at[h], num_rsem.at[h], across(j),
                ).start()
                remote(
                    den_t.at[:, span], den_recv.at[j - 1, :, span],
                    den_send.at[h], den_rsem.at[h], across(j),
                ).start()
    flush()
    pot_ref[...] = jnp.log(source_count * c_buf[1])
    last = []
    for h in range(2):
        span = pl.ds(h * half, half)
        num_copy = remote(
            num_t.at[rest, :, span], num_recv.at[:, :, span],
            num_send.at[h], num_rsem.at[h], across(1),
        )
        den_copy = remote(
            den_recv.at[:, :, span], den_recv.at[:, :, span],
            den_send.at[h], den_rsem.at[h], across(1),
        )
        den_copy.wait_recv()
        den_total = den_t[:, span]
        for j in range(TGT - 1):
            den_total = den_total + den_recv[j, :, span]
        num_copy.wait_recv()
        num_total = num_t[me_t, :, span]
        for j in range(TGT - 1):
            num_total = num_total + num_recv[j, :, span]
        map_ref[:, span] = num_total / den_total
        last += [num_copy, den_copy]
    for copy in last:
        copy.wait_send()


def on_device(source_items, target_items, source_mass, target_mass):
    source_count = source_items.shape[0] * lax.axis_size("src")
    any_spec = pl.BlockSpec(memory_space=pl.ANY)
    vmem_spec = pl.BlockSpec(memory_space=pltpu.VMEM)
    vmem, dma = pltpu.VMEM, pltpu.SemaphoreType.DMA
    mapped, potential = pl.pallas_call(
        functools.partial(kernel, float(source_count)),
        out_shape=(
            jax.ShapeDtypeStruct((SLIVER, ROWS), F32),
            jax.ShapeDtypeStruct((TEAM, 1, PART), F32),
        ),
        in_specs=[any_spec] * 4,
        out_specs=(vmem_spec, vmem_spec),
        scratch_shapes=[
            vmem((ROWS, EMBED), BF16),
            vmem((TEAM, PART, 2 * EMBED), BF16),
            vmem((1, ROWS), F32),
            vmem((TEAM, 1, PART), F32),
            vmem((TEAM, ROWS, PART), F32),
            vmem((2, TEAM, 1, PART), F32),
            vmem((2, TEAM - 1, 1, PART), F32),
            vmem((2, DEPTH, 1, PART), F32),
            vmem((2, TEAM, 1, PART), F32),
            vmem((ROWS, 128), F32),
            vmem((TGT, 1, ROWS), F32),
            vmem((ROWS, 128), F32),
            vmem((ROWS, 2 * EMBED), F32),
            vmem((TGT, SLIVER, ROWS), F32),
            vmem((TGT - 1, SLIVER, ROWS), F32),
            vmem((1, ROWS), F32),
            vmem((TGT - 1, 1, ROWS), F32),
            dma((4,)),
            dma((2,)),
            dma((2,)),
            dma((2,)),
            dma((2,)),
            dma((2,)),
            dma((2, TEAM)),
            dma,
            dma,
            dma((2,)),
            dma((2,)),
            dma((2,)),
            dma((2,)),
        ],
        compiler_params=pltpu.CompilerParams(
            collective_id=0,
            has_side_effects=True,
            vmem_limit_bytes=40 * 1024 * 1024,
        ),
    )(
        source_items,
        target_items.reshape(TEAM, PART, EMBED),
        source_mass.reshape(1, ROWS),
        target_mass.reshape(TEAM, 1, PART),
    )
    return mapped.T, potential.reshape(COLS)


def solution(mesh):
    in_specs = (P("src", None), P("tgt", None), P("src"), P("tgt"))
    out_specs = (P("src", "tgt"), P("tgt"))
    return jax.shard_map(
        on_device, mesh=mesh, in_specs=in_specs, out_specs=out_specs, check_vma=False
    )
```

time: 984 us -> 67.3 us (0.07)
  blocking collectives: 866 us -> 0 us
  Pallas kernels: 0 us -> 61.7 us
  waiting for transfers between devices: 61.4 us -> 0 us
  matrix products: 32.2 us -> 0 us
  between operations: 14.1 us -> 0.65 us
    psum x4 -> x0, blocking collectives: 866 us -> none  [the longest x2 838 us: on_device(): col_total = lax.psum(col_part, 'src')]
    pallas_call x0 -> x1, Pallas kernels: none -> 61.7 us  [on_device(): pl.pallas_call(functools.partial(kernel, float(source_count)), out_shape=...]
    psum x1 -> x0, waiting for transfers between devices: 61.4 us -> none  [on_device(): num_total, den_total = lax.psum((numerator, denominator), 'tgt')]
    dot_general x6 -> x0, matrix products: 32.2 us -> none  [the longest x2 10.4 us: on_device(): col_part = jnp.dot(row_scale, kernel_tile, precision=lax.Precision.HIGHEST)]
  transfers between devices with their start and end apart: 1 -> 0, of which waited for: 1 -> 0; matrix products, arithmetic and copies ran while one was open for 0% -> 0% of each run, Pallas kernels for 0% -> 0%
where the time goes in v1:
time: 67.3 us; the launch traced here: 67.1 us
  Pallas kernels  61.7 us (92%)
  local copies, waits for them, and re-layouts  4.74 us (7%)
    pallas_call x1, Pallas kernels, on_device(): pl.pallas_call(functools.partial(kernel, float(source_count)), out_shape=...  61.7 us
    unnamed x10, local copies, waits for them, and re-layouts  4.74 us

profile of v1, /device:TPU:1, one launch (start us, length us, event | category | flops | bytes accessed | tf_op | source)
XLA Modules:
  0.0 67.1 jit_solution(17019608629308471676)
XLA Ops:
  0.6 0.0 copy-start.3
  0.6 0.7 %copy-done.3 = f32[512]{0:T(512)S(1)} copy-done((f32[512]{0:T(512)S(1)}, f32[512]{0:T(512)}, u32[]{:S(2)}) %copy-start.3) | copy-done | bytes 2072
  1.3 0.0 copy-start
  1.3 1.2 %copy-done = bf16[4096,128]{1,0:T(8,128)(2,1)S(1)} copy-done((bf16[4096,128]{1,0:T(8,128)(2,1)S(1)}, bf16[4096,128]{1,0:T(8,128)(2,1)}, u32[]{:S(2)}) %copy-start) | copy-done | bytes 1048600
  2.5 0.0 copy-start.1
  2.5 0.9 %copy-done.1 = bf16[512,128]{1,0:T(8,128)(2,1)S(1)} copy-done((bf16[512,128]{1,0:T(8,128)(2,1)S(1)}, bf16[512,128]{1,0:T(8,128)(2,1)}, u32[]{:S(2)}) %copy-start.1) | copy-done | bytes 131096
  3.4 0.0 copy-start.2
  3.4 0.7 %copy-done.2 = f32[4096]{0:T(1024)S(1)} copy-done((f32[4096]{0:T(1024)S(1)}, f32[4096]{0:T(1024)}, u32[]{:S(2)}) %copy-start.2) | copy-done | bytes 16408
  4.2 61.7 %shard_map.59 = (f32[16,512]{1,0:T(8,128)S(1)}, f32[8,1,512]{2,1,0:T(1,128)S(1)}) custom-call(bf16[512,128]{1,0:T(8,128)(2,1)S(1)} %copy-done.1, bf16[8,512,128]{2,1,0:T(8,128)(2,1)S(1)} %bitcast.5, f32[1,512]{1,0:T(1,128)S(1)} %bitcast.9, f32[8,1,512]{2,1,0:T(1,128)S(1)} %bitcast.7), custom_call_target="tpu_custom_call" | custom-call | tf_op jit(solution)/shard_map/pallas_call | solution.py:267
  65.8 0.6 copy.8
  66.5 0.6 copy.9
Async XLA Ops:
  0.6 0.7 %copy-start.3 = (f32[512]{0:T(512)S(1)}, f32[512]{0:T(512)}, u32[]{:S(2)}) copy-start(f32[512]{0:T(512)} %param.6) | copy-start | bytes 6148
  1.3 1.2 %copy-start = (bf16[4096,128]{1,0:T(8,128)(2,1)S(1)}, bf16[4096,128]{1,0:T(8,128)(2,1)}, u32[]{:S(2)}) copy-start(bf16[4096,128]{1,0:T(8,128)(2,1)} %param.5) | copy-start | bytes 3145732
  2.5 0.9 %copy-start.1 = (bf16[512,128]{1,0:T(8,128)(2,1)S(1)}, bf16[512,128]{1,0:T(8,128)(2,1)}, u32[]{:S(2)}) copy-start(bf16[512,128]{1,0:T(8,128)(2,1)} %s_hbm.1) | copy-start | bytes 393220
  3.4 0.7 %copy-start.2 = (f32[4096]{0:T(1024)S(1)}, f32[4096]{0:T(1024)}, u32[]{:S(2)}) copy-start(f32[4096]{0:T(1024)} %param.7) | copy-start | bytes 49156

commit v2 on v0

v2 whole, which is shorter than its diff:
```python
import functools
import math

import jax
import jax.numpy as jnp
from jax import lax
from jax.experimental import pallas as pl
from jax.experimental.pallas import tpu as pltpu
from jax.sharding import PartitionSpec as P

ROWS = 512
COLS = 4096
EMBED = 128
RING = 4
DEPTH = 12
PAIR = 2
HALF = COLS // PAIR
LANES = 128
TILES = HALF // LANES
TGT = 8
SLIVER = EMBED // TGT
SPAN = 256
MESH = pl.DeviceIdType.MESH
F32 = jnp.float32
BF16 = jnp.bfloat16
RING_STEPS = (2, 1, 3)
DEPTH_STEPS = (6, 5, 7, 4, 8, 3, 9, 2, 10, 1, 11)
TGT_STEPS = ((2, 1), (2, 0), (1, 1), (3, 1), (1, 0), (3, 0), (0, 1))


def kernel(
    source_count,
    s_hbm, t_hbm, rmass_hbm, cmass_hbm,
    map_ref, pot_ref,
    s_v, text, rmass, cmass, kmat,
    part, half_out, half_in, y_buf, z_buf, c_buf,
    row_acc, row_buf, row_scale, row_wide,
    num, num_t, num_recv, den_t, den_recv,
    load_sem, enter_sem, half_send, half_recv, y_send, y_recv, z_send, z_recv,
    c_send, c_recv, row_send, row_recv, num_send, num_rsem, den_send, den_rsem,
):
    me_s, me_t = lax.axis_index("src"), lax.axis_index("tgt")
    core = lax.rem(me_s, PAIR)
    chip = lax.div(me_s, PAIR)
    zed = lax.rem(chip, DEPTH)
    ring = lax.div(chip, DEPTH)
    twin = 1 - core
    place_x, place_y = lax.div(me_t, 2), lax.rem(me_t, 2)

    def source(ring_at, zed_at, core_at):
        return (ring_at * DEPTH + zed_at) * PAIR + core_at

    twin_id = (source(ring, zed, twin), me_t)
    ring_ids = [(source(lax.rem(ring + k, RING), zed, core), me_t) for k in RING_STEPS]
    depth_at = [lax.rem(zed + k, DEPTH) for k in DEPTH_STEPS]
    depth_ids = [(source(ring, there, core), me_t) for there in depth_at]
    tgt_at = [
        lax.rem(place_x + dx, 4) * 2 + lax.rem(place_y + dy, 2) for dx, dy in TGT_STEPS
    ]
    same_ids = [(me_s, there) for there in tgt_at]

    quarter = HALF // 2
    loads = [pltpu.make_async_copy(s_hbm, s_v, load_sem.at[0])]
    for i, (side, owner) in enumerate(((1, twin), (1, twin), (0, core), (0, core))):
        span = pl.ds(i % 2 * quarter, quarter)
        loads.append(
            pltpu.make_async_copy(
                t_hbm.at[owner, span, :],
                text.at[side, span, pl.ds(0, EMBED)],
                load_sem.at[i + 1],
            )
        )
    loads += [
        pltpu.make_async_copy(rmass_hbm, rmass, load_sem.at[5]),
        pltpu.make_async_copy(cmass_hbm.at[core], cmass, load_sem.at[6]),
    ]
    for load in loads:
        load.start()

    barrier = pltpu.get_barrier_semaphore()
    friends = ring_ids + same_ids + [twin_id]
    for friend in friends:
        pl.semaphore_signal(barrier, inc=1, device_id=friend, device_id_type=MESH)
    for there, friend in zip(depth_at, depth_ids):

        @pl.when(there > zed)
        def _():
            pl.semaphore_signal(barrier, inc=1, device_id=friend, device_id_type=MESH)

    def remote(src, dst, send, recv, where):
        return pltpu.make_async_remote_copy(
            src_ref=src, dst_ref=dst, send_sem=send, recv_sem=recv,
            device_id=where, device_id_type=MESH,
        )

    log2e = 1.4426950408889634
    factor = 2.0 / math.sqrt(EMBED) * log2e
    block = 256

    def kernel_piece(side, piece, sums_ref):
        sums = None
        for m in range(ROWS // block):
            logits = lax.dot_general(
                s_v[pl.ds(m * block, block), :],
                text[side, pl.ds(piece * 256, 256), pl.ds(0, EMBED)],
                (((1,), (1,)), ((), ())), preferred_element_type=F32,
            )
            tile = jnp.exp2(logits * factor)
            for i in range(2):
                kmat[side, piece * 2 + i, pl.ds(m * block, block), :] = tile[
                    :, i * LANES : (i + 1) * LANES
                ]
            term = jnp.sum(tile.reshape(block // 8, 8, 256), axis=0)
            sums = term if sums is None else sums + term
        sums = jnp.sum(sums, axis=0, keepdims=True)
        for i in range(2):
            sums_ref[pl.ds(piece * 2 + i, 1), :] = sums[:, i * LANES : (i + 1) * LANES]

    def half_copy(it):
        return remote(
            half_out.at[it], half_in.at[it], half_send.at[it], half_recv.at[it], twin_id
        )

    loads[0].wait()
    pieces = HALF // 256
    for piece in range(pieces):
        if piece % (pieces // 2) == 0:
            loads[1 + piece // (pieces // 2)].wait()
        kernel_piece(1, piece, half_out.at[0])
    for piece in range(pieces):
        if piece % (pieces // 2) == 0:
            loads[3 + piece // (pieces // 2)].wait()
        if piece == pieces // 2:
            pl.semaphore_wait(barrier, len(friends) + zed)
            half_copy(0).start()
            for there, friend in zip(depth_at, depth_ids):

                @pl.when(there < zed)
                def _():
                    pl.semaphore_signal(
                        enter_sem, inc=1, device_id=friend, device_id_type=MESH
                    )

        kernel_piece(0, piece, part)

    def finish_columns(it, meanwhile):
        half_copy(it).wait_recv()
        y_buf[it, ring] = part[...] + half_in[it]
        for where in ring_ids:
            remote(
                y_buf.at[it, ring], y_buf.at[it, ring], y_send.at[it], y_recv.at[it], where
            ).start()
        half_copy(it).wait_send()
        meanwhile()
        others = pl.ds(0, RING - 1)
        trio = remote(
            y_buf.at[it, others], y_buf.at[it, others],
            y_send.at[it], y_recv.at[it], twin_id,
        )
        trio.wait_recv()
        total = y_buf[it, 0]
        for k in range(1, RING):
            total = total + y_buf[it, k]
        z_buf[it, zed] = total

        def send_depth(where):
            remote(
                z_buf.at[it, zed], z_buf.at[it, zed], z_send.at[it], z_recv.at[it], where
            ).start()

        if it == 0:
            for there, where in zip(depth_at, depth_ids):

                @pl.when(there < zed)
                def _():
                    send_depth(where)

            @pl.when(zed < DEPTH - 1)
            def _():
                pl.semaphore_wait(enter_sem, DEPTH - 1 - zed)

            for there, where in zip(depth_at, depth_ids):

                @pl.when(there > zed)
                def _():
                    send_depth(where)

        else:
            for where in depth_ids:
                send_depth(where)
        trio.wait_send()
        others = pl.ds(0, DEPTH - 1)
        column = remote(
            z_buf.at[it, others], z_buf.at[it, others],
            z_send.at[it], z_recv.at[it], twin_id,
        )
        column.wait_recv()
        total = z_buf[it, 0]
        for k in range(1, DEPTH):
            total = total + z_buf[it, k]
        c_buf[it, 0] = cmass[...] / total
        mirror = remote(
            c_buf.at[it, 0], c_buf.at[it, 1], c_send.at[it], c_recv.at[it], twin_id
        )
        mirror.start()
        return column, mirror

    def first_wait():
        text[:, :, pl.ds(EMBED, EMBED)] = jnp.ones((PAIR, HALF, EMBED), BF16)
        for load in loads[5:]:
            load.wait()

    column, mirror = finish_columns(0, first_wait)

    step = 64
    for side in range(PAIR):
        if side == 1:
            column.wait_send()
            mirror.wait_recv()
        for b in range(ROWS // step):
            span = pl.ds(b * step, step)
            fold = kmat[side, 0, span, :] * c_buf[0, side, pl.ds(0, 1), :]
            for r in range(1, TILES):
                fold = fold + kmat[side, r, span, :] * c_buf[0, side, pl.ds(r, 1), :]
            if side == 1:
                fold = fold + row_acc[span, :]
            row_acc[span, :] = fold
    for i in range(ROWS // LANES):
        row_buf[me_t, pl.ds(i, 1), :] = jnp.sum(
            row_acc[pl.ds(i * LANES, LANES), :].T, axis=0, keepdims=True
        )
    for where in same_ids:
        remote(
            row_buf.at[me_t], row_buf.at[me_t], row_send, row_recv, where
        ).start()
    mirror.wait_send()
    rest = pl.ds(0, TGT - 1)
    rows = remote(row_buf.at[rest], row_buf.at[rest], row_send, row_recv, twin_id)
    rows.wait_recv()
    total = row_buf[0]
    for k in range(1, TGT):
        total = total + row_buf[k]
    row_scale[...] = rmass[...] / total
    for i in range(ROWS // LANES):
        wide = jnp.broadcast_to(row_scale[pl.ds(i, 1), :], (LANES, LANES))
        row_wide[pl.ds(i * LANES, LANES), :] = wide.T

    for side, sums_ref in ((1, half_out.at[1]), (0, part)):
        sums = [jnp.zeros((8, LANES), F32)] * TILES
        for b in range(ROWS // step):
            span = pl.ds(b * step, step)
            wide = row_wide[span, :]
            for r in range(TILES):
                term = (kmat[side, r, span, :] * wide).reshape(step // 8, 8, LANES)
                sums[r] = sums[r] + jnp.sum(term, axis=0)
        for r in range(TILES):
            sums_ref[pl.ds(r, 1), :] = jnp.sum(sums[r], axis=0, keepdims=True)
        if side == 1:
            half_copy(1).start()

    column, mirror = finish_columns(1, rows.wait_send)

    def weighted(side, span):
        weights = jnp.concatenate(
            [
                (kmat[side, r, span, :] * c_buf[1, side, pl.ds(r, 1), :]).astype(BF16)
                for r in range(TILES)
            ],
            axis=1,
        )
        return jnp.dot(weights, text[side], preferred_element_type=F32)

    for h in range(ROWS // SPAN):
        span = pl.ds(h * SPAN, SPAN)
        num[span, :] = weighted(0, span)
    mirror.wait_recv()
    for h in range(ROWS // SPAN):
        span = pl.ds(h * SPAN, SPAN)
        term = weighted(1, span) + num[span, :]
        num_t[:, :, span] = term[:, :EMBED].T.reshape(TGT, SLIVER, SPAN)
        den_t[:, span] = term[:, EMBED:].T[:1]
        for j, there in enumerate(tgt_at):
            remote(
                num_t.at[there, :, span], num_recv.at[j, :, span],
                num_send.at[h], num_rsem.at[h], same_ids[j],
            ).start()
    for j in range(TGT - 1):
        remote(den_t, den_recv.at[j], den_send, den_rsem, same_ids[j]).start()

    pot_ref[core] = jnp.log(source_count * c_buf[1, 0])
    pot_ref[twin] = jnp.log(source_count * c_buf[1, 1])
    column.wait_send()
    mirror.wait_send()
    last = []
    for h in range(ROWS // SPAN):
        span = pl.ds(h * SPAN, SPAN)
        last.append(
            remote(
                num_t.at[pl.ds(0, TGT - 1), :, span], num_recv.at[:, :, span],
                num_send.at[h], num_rsem.at[h], twin_id,
            )
        )
    den_copy = remote(den_recv, den_recv, den_send, den_rsem, twin_id)
    den_copy.wait_recv()
    den_total = den_t[...]
    for j in range(TGT - 1):
        den_total = den_total + den_recv[j]
    for h in range(ROWS // SPAN):
        span = pl.ds(h * SPAN, SPAN)
        last[h].wait_recv()
        num_total = num_t[me_t, :, span]
        for j in range(TGT - 1):
            num_total = num_total + num_recv[j, :, span]
        map_ref[:, span] = num_total / den_total[:, h * SPAN : (h + 1) * SPAN]
    for copy in last + [den_copy]:
        copy.wait_send()


def on_device(source_items, target_items, source_mass, target_mass):
    source_count = source_items.shape[0] * lax.axis_size("src")
    any_spec = pl.BlockSpec(memory_space=pltpu.HBM)
    vmem_spec = pl.BlockSpec(memory_space=pltpu.VMEM)
    vmem, dma = pltpu.VMEM, pltpu.SemaphoreType.DMA
    mapped, potential = pl.pallas_call(
        functools.partial(kernel, float(source_count)),
        out_shape=(
            jax.ShapeDtypeStruct((SLIVER, ROWS), F32),
            jax.ShapeDtypeStruct((PAIR, TILES, LANES), F32),
        ),
        in_specs=[any_spec] * 4,
        out_specs=(vmem_spec, vmem_spec),
        scratch_shapes=[
            vmem((ROWS, EMBED), BF16),
            vmem((PAIR, HALF, 2 * EMBED), BF16),
            vmem((ROWS // LANES, LANES), F32),
            vmem((TILES, LANES), F32),
            vmem((PAIR, TILES, ROWS, LANES), F32),
            vmem((TILES, LANES), F32),
            vmem((2, TILES, LANES), F32),
            vmem((2, TILES, LANES), F32),
            vmem((2, RING, TILES, LANES), F32),
            vmem((2, DEPTH, TILES, LANES), F32),
            vmem((2, PAIR, TILES, LANES), F32),
            vmem((ROWS, LANES), F32),
            vmem((TGT, ROWS // LANES, LANES), F32),
            vmem((ROWS // LANES, LANES), F32),
            vmem((ROWS, LANES), F32),
            vmem((ROWS, 2 * EMBED), F32),
            vmem((TGT, SLIVER, ROWS), F32),
            vmem((TGT - 1, SLIVER, ROWS), F32),
            vmem((1, ROWS), F32),
            vmem((TGT - 1, 1, ROWS), F32),
            dma((7,)),
            pltpu.SemaphoreType.REGULAR,
            dma((2,)),
            dma((2,)),
            dma((2,)),
            dma((2,)),
            dma((2,)),
            dma((2,)),
            dma((2,)),
            dma((2,)),
            dma,
            dma,
            dma((ROWS // SPAN,)),
            dma((ROWS // SPAN,)),
            dma,
            dma,
        ],
        compiler_params=pltpu.CompilerParams(
            collective_id=0,
            has_side_effects=True,
            vmem_limit_bytes=56000 * 1024,
        ),
    )(
        source_items,
        target_items.reshape(PAIR, HALF, EMBED),
        source_mass.reshape(ROWS // LANES, LANES),
        target_mass.reshape(PAIR, TILES, LANES),
    )
    return mapped.T, potential.reshape(COLS)


def solution(mesh):
    in_specs = (P("src", None), P("tgt", None), P("src"), P("tgt"))
    out_specs = (P("src", "tgt"), P("tgt"))
    return jax.shard_map(
        on_device, mesh=mesh, in_specs=in_specs, out_specs=out_specs, check_vma=False
    )
```

time: 984 us -> 58.8 us (0.06)
  blocking collectives: 866 us -> 0 us
  waiting for transfers between devices: 61.4 us -> 0 us
  Pallas kernels: 0 us -> 56 us
  matrix products: 32.2 us -> 0 us
  between operations: 14.1 us -> 0.65 us
    psum x4 -> x0, blocking collectives: 866 us -> none  [the longest x2 838 us: on_device(): col_total = lax.psum(col_part, 'src')]
    psum x1 -> x0, waiting for transfers between devices: 61.4 us -> none  [on_device(): num_total, den_total = lax.psum((numerator, denominator), 'tgt')]
    pallas_call x0 -> x1, Pallas kernels: none -> 56 us  [on_device(): pl.pallas_call(functools.partial(kernel, float(source_count)), out_shape=...]
    dot_general x6 -> x0, matrix products: 32.2 us -> none  [the longest x2 10.4 us: on_device(): col_part = jnp.dot(row_scale, kernel_tile, precision=lax.Precision.HIGHEST)]
  transfers between devices with their start and end apart: 1 -> 0, of which waited for: 1 -> 0; matrix products, arithmetic and copies ran while one was open for 0% -> 0% of each run, Pallas kernels for 0% -> 0%
where the time goes in v2:
time: 58.8 us; the launch traced here: 58.6 us
  Pallas kernels  56 us (95%)
  local copies, waits for them, and re-layouts  1.99 us (3%)
  between operations  0.65 us (1%)
    pallas_call x1, Pallas kernels, on_device(): pl.pallas_call(functools.partial(kernel, float(source_count)), out_shape=...  56 us
    unnamed x4, local copies, waits for them, and re-layouts  1.99 us

profile of v2, /device:TPU:1, one launch (start us, length us, event | category | flops | bytes accessed | tf_op | source)
XLA Modules:
  0.0 58.6 jit_solution(17228835903913894759)
XLA Ops:
  0.6 56.0 %shard_map.59 = (f32[16,512]{1,0:T(8,128)}, f32[2,16,128]{2,1,0:T(8,128)}) custom-call(bf16[512,128]{1,0:T(8,128)(2,1)} %s_hbm.1, bf16[2,2048,128]{2,1,0:T(8,128)(2,1)} %bitcast.5, f32[4,128]{1,0:T(4,128)} %bitcast.9, f32[2,16,128]{2,1,0:T(8,128)} %bitcast.7), custom_call_target="tpu_custom_call" | custom-call | tf_op jit(solution)/shard_map/pallas_call | solution.py:324
  56.6 0.0 copy-start
  56.6 1.4 %copy.8 = f32[512,16]{0,1:T(8,128)} copy(f32[512,16]{0,1:T(8,128)} %bitcast.6) | data formatting | bytes 65536
  58.0 0.0 copy-done
  58.0 0.6 %copy.9 = f32[4096]{0:T(1024)} copy(f32[4096]{0:T(1024)S(1)} %bitcast.8) | data formatting | bytes 32768
Async XLA Ops:
  56.6 1.4 %copy-start = (f32[2,16,128]{2,1,0:T(8,128)S(1)}, f32[2,16,128]{2,1,0:T(8,128)}, u32[]{:S(2)}) copy-start(f32[2,16,128]{2,1,0:T(8,128)} %get-tuple-element.5) | copy-start | bytes 49156

commit v3 on v2

--- a/solution.py
+++ b/solution.py
@@ -20,6 +20,7 @@
 TGT = 8
 SLIVER = EMBED // TGT
 SPAN = 256
+LIMIT = 40 * 1024
 MESH = pl.DeviceIdType.MESH
 F32 = jnp.float32
 BF16 = jnp.bfloat16
@@ -316,9 +317,24 @@
         copy.wait_send()
 
 
+def finish(map_in, pot_in, map_out, pot_out, sem):
+    copies = [
+        pltpu.make_async_copy(map_in, map_out, sem.at[0]),
+        pltpu.make_async_copy(pot_in, pot_out, sem.at[1]),
+    ]
+    for copy in copies:
+        copy.start()
+    for copy in copies:
+        copy.wait()
+
+
+def in_hbm(x):
+    return pltpu.with_memory_space_constraint(x, pltpu.HBM)
+
+
 def on_device(source_items, target_items, source_mass, target_mass):
     source_count = source_items.shape[0] * lax.axis_size("src")
-    any_spec = pl.BlockSpec(memory_space=pltpu.HBM)
+    hbm_spec = any_spec = pl.BlockSpec(memory_space=pltpu.HBM)
     vmem_spec = pl.BlockSpec(memory_space=pltpu.VMEM)
     vmem, dma = pltpu.VMEM, pltpu.SemaphoreType.DMA
     mapped, potential = pl.pallas_call(
@@ -370,14 +386,25 @@
         compiler_params=pltpu.CompilerParams(
             collective_id=0,
             has_side_effects=True,
-            vmem_limit_bytes=56000 * 1024,
+            vmem_limit_bytes=LIMIT * 1024,
         ),
     )(
-        source_items,
-        target_items.reshape(PAIR, HALF, EMBED),
-        source_mass.reshape(ROWS // LANES, LANES),
-        target_mass.reshape(PAIR, TILES, LANES),
+        in_hbm(source_items),
+        in_hbm(target_items.reshape(PAIR, HALF, EMBED)),
+        in_hbm(source_mass.reshape(ROWS // LANES, LANES)),
+        in_hbm(target_mass.reshape(PAIR, TILES, LANES)),
     )
+    mapped, potential = pl.pallas_call(
+        finish,
+        out_shape=(
+            jax.ShapeDtypeStruct((SLIVER, ROWS), F32),
+            jax.ShapeDtypeStruct((PAIR, TILES, LANES), F32),
+        ),
+        in_specs=[vmem_spec] * 2,
+        out_specs=(hbm_spec, hbm_spec),
+        scratch_shapes=[dma((2,))],
+        compiler_params=pltpu.CompilerParams(vmem_limit_bytes=LIMIT * 1024),
+    )(mapped, potential)
     return mapped.T, potential.reshape(COLS)
 
 

time: 58.8 us -> 56.9 us (0.968)
  local copies, waits for them, and re-layouts: 1.99 us -> 0 us
    unnamed x4 -> x0, local copies, waits for them, and re-layouts: 1.99 us -> none
    pallas_call x0 -> x1, Pallas kernels: none -> 0.64 us  [on_device(): pl.pallas_call(finish, out_shape=(jax.ShapeDtypeStruct((SLIVER, ROWS), F3...]
where the time goes in v3:
time: 56.9 us; the launch traced here: 56.8 us
  Pallas kernels  56.1 us (99%)
  between operations  0.64 us (1%)
    pallas_call x1, Pallas kernels, on_device(): pl.pallas_call(functools.partial(kernel, float(source_count)), out_shape=...  55.5 us

profile of v3, /device:TPU:1, one launch (start us, length us, event | category | flops | bytes accessed | tf_op | source)
XLA Modules:
  0.0 56.8 jit_solution(16928436845486580938)
XLA Ops:
  0.6 55.5 %shard_map.59 = (f32[16,512]{1,0:T(8,128)S(1)}, f32[2,16,128]{2,1,0:T(8,128)S(1)}) custom-call(bf16[512,128]{1,0:T(8,128)(2,1)} %s_hbm.1, bf16[2,2048,128]{2,1,0:T(8,128)(2,1)} %bitcast.5, f32[4,128]{1,0:T(4,128)} %bitcast.7, f32[2,16,128]{2,1,0:T(8,128)} %bitcast.6), custom_call_target="tpu_custom_call" | custom-call | tf_op jit(solution)/shard_map/pallas_call | solution.py:340
  56.2 0.6 %shard_map.60 = (f32[16,512]{1,0:T(8,128)}, f32[2,16,128]{2,1,0:T(8,128)}) custom-call(f32[16,512]{1,0:T(8,128)S(1)} %get-tuple-element.6.map_in, f32[2,16,128]{2,1,0:T(8,128)S(1)} %get-tuple-element.7.pot_in), custom_call_target="tpu_custom_call" | custom-call | tf_op jit(solution)/shard_map/pallas_call | solution.py:397

commit v4 on v3

--- a/solution.py
+++ b/solution.py
@@ -26,6 +26,7 @@
 BF16 = jnp.bfloat16
 RING_STEPS = (2, 1, 3)
 DEPTH_STEPS = (6, 5, 7, 4, 8, 3, 9, 2, 10, 1, 11)
+DEPTH_ORDER = (0, 1, 2, 3, 11, 4, 10, 5, 9, 6, 8, 7)
 TGT_STEPS = ((2, 1), (2, 0), (1, 1), (3, 1), (1, 0), (3, 0), (0, 1))
 
 
@@ -34,10 +35,10 @@
     s_hbm, t_hbm, rmass_hbm, cmass_hbm,
     map_ref, pot_ref,
     s_v, text, rmass, cmass, kmat,
-    part, half_out, half_in, y_buf, z_buf, c_buf,
+    part, cross_out, y_buf, z_buf, c_buf,
     row_acc, row_buf, row_scale, row_wide,
     num, num_t, num_recv, den_t, den_recv,
-    load_sem, enter_sem, half_send, half_recv, y_send, y_recv, z_send, z_recv,
+    load_sem, enter_sem, y_send, y_recv, z_send, z_recv,
     c_send, c_recv, row_send, row_recv, num_send, num_rsem, den_send, den_rsem,
 ):
     me_s, me_t = lax.axis_index("src"), lax.axis_index("tgt")
@@ -53,6 +54,10 @@
 
     twin_id = (source(ring, zed, twin), me_t)
     ring_ids = [(source(lax.rem(ring + k, RING), zed, core), me_t) for k in RING_STEPS]
+    ring_cross_ids = [
+        (source(lax.rem(ring + k, RING), zed, twin), me_t) for k in RING_STEPS
+    ]
+    berth = ring * PAIR + core
     depth_at = [lax.rem(zed + k, DEPTH) for k in DEPTH_STEPS]
     depth_ids = [(source(ring, there, core), me_t) for there in depth_at]
     tgt_at = [
@@ -79,7 +84,7 @@
         load.start()
 
     barrier = pltpu.get_barrier_semaphore()
-    friends = ring_ids + same_ids + [twin_id]
+    friends = ring_ids + ring_cross_ids + same_ids + [twin_id]
     for friend in friends:
         pl.semaphore_signal(barrier, inc=1, device_id=friend, device_id_type=MESH)
     for there, friend in zip(depth_at, depth_ids):
@@ -117,50 +122,43 @@
         for i in range(2):
             sums_ref[pl.ds(piece * 2 + i, 1), :] = sums[:, i * LANES : (i + 1) * LANES]
 
-    def half_copy(it):
-        return remote(
-            half_out.at[it], half_in.at[it], half_send.at[it], half_recv.at[it], twin_id
-        )
+    def ring_start(it, same):
+        src = y_buf.at[it, berth] if same else cross_out.at[it]
+        for where in ring_ids if same else ring_cross_ids + [twin_id]:
+            remote(
+                src, y_buf.at[it, berth], y_send.at[it], y_recv.at[it], where
+            ).start()
 
     loads[0].wait()
     pieces = HALF // 256
     for piece in range(pieces):
         if piece % (pieces // 2) == 0:
             loads[1 + piece // (pieces // 2)].wait()
-        kernel_piece(1, piece, half_out.at[0])
+        kernel_piece(1, piece, cross_out.at[0])
     for piece in range(pieces):
         if piece % (pieces // 2) == 0:
             loads[3 + piece // (pieces // 2)].wait()
-        if piece == pieces // 2:
-            pl.semaphore_wait(barrier, len(friends) + zed)
-            half_copy(0).start()
-            for there, friend in zip(depth_at, depth_ids):
-
-                @pl.when(there < zed)
-                def _():
-                    pl.semaphore_signal(
-                        enter_sem, inc=1, device_id=friend, device_id_type=MESH
-                    )
-
         kernel_piece(0, piece, part)
+    y_buf[0, berth] = part[...]
+    pl.semaphore_wait(barrier, len(friends) + zed)
+    ring_start(0, False)
+    ring_start(0, True)
+    for there, friend in zip(depth_at, depth_ids):
+
+        @pl.when(there < zed)
+        def _():
+            pl.semaphore_signal(enter_sem, inc=1, device_id=friend, device_id_type=MESH)
 
     def finish_columns(it, meanwhile):
-        half_copy(it).wait_recv()
-        y_buf[it, ring] = part[...] + half_in[it]
-        for where in ring_ids:
-            remote(
-                y_buf.at[it, ring], y_buf.at[it, ring], y_send.at[it], y_recv.at[it], where
-            ).start()
-        half_copy(it).wait_send()
         meanwhile()
-        others = pl.ds(0, RING - 1)
+        others = pl.ds(0, PAIR * RING - 1)
         trio = remote(
             y_buf.at[it, others], y_buf.at[it, others],
             y_send.at[it], y_recv.at[it], twin_id,
         )
         trio.wait_recv()
         total = y_buf[it, 0]
-        for k in range(1, RING):
+        for k in range(1, PAIR * RING):
             total = total + y_buf[it, k]
         z_buf[it, zed] = total
 
@@ -187,8 +185,12 @@
                     send_depth(where)
 
         else:
-            for where in depth_ids:
-                send_depth(where)
+            for there in DEPTH_ORDER:
+
+                @pl.when(zed != there)
+                def _():
+                    send_depth((source(ring, there, core), me_t))
+
         trio.wait_send()
         others = pl.ds(0, DEPTH - 1)
         column = remote(
@@ -246,7 +248,7 @@
         wide = jnp.broadcast_to(row_scale[pl.ds(i, 1), :], (LANES, LANES))
         row_wide[pl.ds(i * LANES, LANES), :] = wide.T
 
-    for side, sums_ref in ((1, half_out.at[1]), (0, part)):
+    for side, sums_ref in ((1, cross_out.at[1]), (0, part)):
         sums = [jnp.zeros((8, LANES), F32)] * TILES
         for b in range(ROWS // step):
             span = pl.ds(b * step, step)
@@ -256,8 +258,9 @@
                 sums[r] = sums[r] + jnp.sum(term, axis=0)
         for r in range(TILES):
             sums_ref[pl.ds(r, 1), :] = jnp.sum(sums[r], axis=0, keepdims=True)
-        if side == 1:
-            half_copy(1).start()
+        if side == 0:
+            y_buf[1, berth] = part[...]
+        ring_start(1, side == 0)
 
     column, mirror = finish_columns(1, rows.wait_send)
 
@@ -353,8 +356,7 @@
             vmem((PAIR, TILES, ROWS, LANES), F32),
             vmem((TILES, LANES), F32),
             vmem((2, TILES, LANES), F32),
-            vmem((2, TILES, LANES), F32),
-            vmem((2, RING, TILES, LANES), F32),
+            vmem((2, PAIR * RING, TILES, LANES), F32),
             vmem((2, DEPTH, TILES, LANES), F32),
             vmem((2, PAIR, TILES, LANES), F32),
             vmem((ROWS, LANES), F32),
@@ -368,8 +370,6 @@
             vmem((TGT - 1, 1, ROWS), F32),
             dma((7,)),
             pltpu.SemaphoreType.REGULAR,
-            dma((2,)),
-            dma((2,)),
             dma((2,)),
             dma((2,)),
             dma((2,)),

time: 56.9 us -> 55.6 us (0.977)
  Pallas kernels: 56.1 us -> 54.8 us
    pallas_call x1, Pallas kernels: 55.5 us -> 54.1 us  [on_device(): pl.pallas_call(functools.partial(kernel, float(source_count)), out_shape=...]
where the time goes in v4:
time: 55.6 us; the launch traced here: 55.4 us
  Pallas kernels  54.8 us (99%)
  between operations  0.64 us (1%)
    pallas_call x1, Pallas kernels, on_device(): pl.pallas_call(functools.partial(kernel, float(source_count)), out_shape=...  54.1 us

profile of v4, /device:TPU:1, one launch (start us, length us, event | category | flops | bytes accessed | tf_op | source)
XLA Modules:
  0.0 55.4 jit_solution(12300429422635205334)
XLA Ops:
  0.6 54.1 %shard_map.59 = (f32[16,512]{1,0:T(8,128)S(1)}, f32[2,16,128]{2,1,0:T(8,128)S(1)}) custom-call(bf16[512,128]{1,0:T(8,128)(2,1)} %s_hbm.1, bf16[2,2048,128]{2,1,0:T(8,128)(2,1)} %bitcast.5, f32[4,128]{1,0:T(4,128)} %bitcast.7, f32[2,16,128]{2,1,0:T(8,128)} %bitcast.6), custom_call_target="tpu_custom_call" | custom-call | tf_op jit(solution)/shard_map/pallas_call | solution.py:343
  54.8 0.6 %shard_map.60 = (f32[16,512]{1,0:T(8,128)}, f32[2,16,128]{2,1,0:T(8,128)}) custom-call(f32[16,512]{1,0:T(8,128)S(1)} %get-tuple-element.6.map_in, f32[2,16,128]{2,1,0:T(8,128)S(1)} %get-tuple-element.7.pot_in), custom_call_target="tpu_custom_call" | custom-call | tf_op jit(solution)/shard_map/pallas_call | solution.py:397

commit v5 on v4

--- a/solution.py
+++ b/solution.py
@@ -288,8 +288,8 @@
                 num_t.at[there, :, span], num_recv.at[j, :, span],
                 num_send.at[h], num_rsem.at[h], same_ids[j],
             ).start()
-    for j in range(TGT - 1):
-        remote(den_t, den_recv.at[j], den_send, den_rsem, same_ids[j]).start()
+            if h == ROWS // SPAN - 1:
+                remote(den_t, den_recv.at[j], den_send, den_rsem, same_ids[j]).start()
 
     pot_ref[core] = jnp.log(source_count * c_buf[1, 0])
     pot_ref[twin] = jnp.log(source_count * c_buf[1, 1])

time: 55.6 us -> 55.2 us (level)
  no operation moved by 1% of the time
where the time goes in v5:
time: 55.2 us; the launch traced here: 55.1 us
  Pallas kernels  54.4 us (99%)
  between operations  0.64 us (1%)
    pallas_call x1, Pallas kernels, on_device(): pl.pallas_call(functools.partial(kernel, float(source_count)), out_shape=...  53.8 us

profile of v5, /device:TPU:1, one launch (start us, length us, event | category | flops | bytes accessed | tf_op | source)
XLA Modules:
  0.0 55.1 jit_solution(8804000941570974247)
XLA Ops:
  0.6 53.8 %shard_map.59 = (f32[16,512]{1,0:T(8,128)S(1)}, f32[2,16,128]{2,1,0:T(8,128)S(1)}) custom-call(bf16[512,128]{1,0:T(8,128)(2,1)} %s_hbm.1, bf16[2,2048,128]{2,1,0:T(8,128)(2,1)} %bitcast.5, f32[4,128]{1,0:T(4,128)} %bitcast.7, f32[2,16,128]{2,1,0:T(8,128)} %bitcast.6), custom_call_target="tpu_custom_call" | custom-call | tf_op jit(solution)/shard_map/pallas_call | solution.py:343
  54.4 0.6 %shard_map.60 = (f32[16,512]{1,0:T(8,128)}, f32[2,16,128]{2,1,0:T(8,128)}) custom-call(f32[16,512]{1,0:T(8,128)S(1)} %get-tuple-element.6.map_in, f32[2,16,128]{2,1,0:T(8,128)S(1)} %get-tuple-element.7.pot_in), custom_call_target="tpu_custom_call" | custom-call | tf_op jit(solution)/shard_map/pallas_call | solution.py:397

commit v6 on v5

--- a/solution.py
+++ b/solution.py
@@ -26,7 +26,6 @@
 BF16 = jnp.bfloat16
 RING_STEPS = (2, 1, 3)
 DEPTH_STEPS = (6, 5, 7, 4, 8, 3, 9, 2, 10, 1, 11)
-DEPTH_ORDER = (0, 1, 2, 3, 11, 4, 10, 5, 9, 6, 8, 7)
 TGT_STEPS = ((2, 1), (2, 0), (1, 1), (3, 1), (1, 0), (3, 0), (0, 1))
 
 
@@ -122,12 +121,9 @@
         for i in range(2):
             sums_ref[pl.ds(piece * 2 + i, 1), :] = sums[:, i * LANES : (i + 1) * LANES]
 
-    def ring_start(it, same):
+    def ring_send(it, same, where):
         src = y_buf.at[it, berth] if same else cross_out.at[it]
-        for where in ring_ids if same else ring_cross_ids + [twin_id]:
-            remote(
-                src, y_buf.at[it, berth], y_send.at[it], y_recv.at[it], where
-            ).start()
+        remote(src, y_buf.at[it, berth], y_send.at[it], y_recv.at[it], where).start()
 
     loads[0].wait()
     pieces = HALF // 256
@@ -141,8 +137,10 @@
         kernel_piece(0, piece, part)
     y_buf[0, berth] = part[...]
     pl.semaphore_wait(barrier, len(friends) + zed)
-    ring_start(0, False)
-    ring_start(0, True)
+    for same_id, cross_id in zip(ring_ids, ring_cross_ids):
+        ring_send(0, False, cross_id)
+        ring_send(0, True, same_id)
+    ring_send(0, False, twin_id)
     for there, friend in zip(depth_at, depth_ids):
 
         @pl.when(there < zed)
@@ -185,11 +183,9 @@
                     send_depth(where)
 
         else:
-            for there in DEPTH_ORDER:
-
-                @pl.when(zed != there)
-                def _():
-                    send_depth((source(ring, there, core), me_t))
+            for j in range(DEPTH - 1):
+                there = jnp.where(zed <= j, j + 1, j)
+                send_depth((source(ring, there, core), me_t))
 
         trio.wait_send()
         others = pl.ds(0, DEPTH - 1)
@@ -260,7 +256,8 @@
             sums_ref[pl.ds(r, 1), :] = jnp.sum(sums[r], axis=0, keepdims=True)
         if side == 0:
             y_buf[1, berth] = part[...]
-        ring_start(1, side == 0)
+        for where in ring_cross_ids + [twin_id] if side else ring_ids:
+            ring_send(1, side == 0, where)
 
     column, mirror = finish_columns(1, rows.wait_send)
 
@@ -274,9 +271,7 @@
         )
         return jnp.dot(weights, text[side], preferred_element_type=F32)
 
-    for h in range(ROWS // SPAN):
-        span = pl.ds(h * SPAN, SPAN)
-        num[span, :] = weighted(0, span)
+    num[...] = weighted(0, pl.ds(0, ROWS))
     mirror.wait_recv()
     for h in range(ROWS // SPAN):
         span = pl.ds(h * SPAN, SPAN)
@@ -305,16 +300,21 @@
             )
         )
     den_copy = remote(den_recv, den_recv, den_send, den_rsem, twin_id)
-    den_copy.wait_recv()
-    den_total = den_t[...]
-    for j in range(TGT - 1):
-        den_total = den_total + den_recv[j]
+    totals = []
     for h in range(ROWS // SPAN):
+        if h == ROWS // SPAN - 1:
+            den_copy.wait_recv()
+            den_total = den_t[...]
+            for j in range(TGT - 1):
+                den_total = den_total + den_recv[j]
         span = pl.ds(h * SPAN, SPAN)
         last[h].wait_recv()
         num_total = num_t[me_t, :, span]
         for j in range(TGT - 1):
             num_total = num_total + num_recv[j, :, span]
+        totals.append(num_total)
+    for h, num_total in enumerate(totals):
+        span = pl.ds(h * SPAN, SPAN)
         map_ref[:, span] = num_total / den_total[:, h * SPAN : (h + 1) * SPAN]
     for copy in last + [den_copy]:
         copy.wait_send()

time: 55.2 us -> 55 us (level)
  no operation moved by 1% of the time
where the time goes in v6:
time: 55 us; the launch traced here: 54.8 us
  Pallas kernels  54.2 us (99%)
  between operations  0.64 us (1%)
    pallas_call x1, Pallas kernels, on_device(): pl.pallas_call(functools.partial(kernel, float(source_count)), out_shape=...  53.5 us

profile of v6, /device:TPU:1, one launch (start us, length us, event | category | flops | bytes accessed | tf_op | source)
XLA Modules:
  0.0 54.8 jit_solution(18171675320099783409)
XLA Ops:
  0.6 53.5 %shard_map.59 = (f32[16,512]{1,0:T(8,128)S(1)}, f32[2,16,128]{2,1,0:T(8,128)S(1)}) custom-call(bf16[512,128]{1,0:T(8,128)(2,1)} %s_hbm.1, bf16[2,2048,128]{2,1,0:T(8,128)(2,1)} %bitcast.5, f32[4,128]{1,0:T(4,128)} %bitcast.7, f32[2,16,128]{2,1,0:T(8,128)} %bitcast.6), custom_call_target="tpu_custom_call" | custom-call | tf_op jit(solution)/shard_map/pallas_call | solution.py:343
  54.2 0.6 %shard_map.60 = (f32[16,512]{1,0:T(8,128)}, f32[2,16,128]{2,1,0:T(8,128)}) custom-call(f32[16,512]{1,0:T(8,128)S(1)} %get-tuple-element.6.map_in, f32[2,16,128]{2,1,0:T(8,128)S(1)} %get-tuple-element.7.pot_in), custom_call_target="tpu_custom_call" | custom-call | tf_op jit(solution)/shard_map/pallas_call | solution.py:397

commit v7 on v6

--- a/solution.py
+++ b/solution.py
@@ -211,7 +211,7 @@
 
     column, mirror = finish_columns(0, first_wait)
 
-    step = 64
+    step = 128
     for side in range(PAIR):
         if side == 1:
             column.wait_send()

time: 55 us -> 54.6 us (level)
  no operation moved by 1% of the time
where the time goes in v7:
time: 54.6 us; the launch traced here: 54.5 us
  Pallas kernels  53.8 us (99%)
  between operations  0.64 us (1%)
    pallas_call x1, Pallas kernels, on_device(): pl.pallas_call(functools.partial(kernel, float(source_count)), out_shape=...  53.2 us

profile of v7, /device:TPU:1, one launch (start us, length us, event | category | flops | bytes accessed | tf_op | source)
XLA Modules:
  0.0 54.5 jit_solution(1643042721773145452)
XLA Ops:
  0.6 53.2 %shard_map.59 = (f32[16,512]{1,0:T(8,128)S(1)}, f32[2,16,128]{2,1,0:T(8,128)S(1)}) custom-call(bf16[512,128]{1,0:T(8,128)(2,1)} %s_hbm.1, bf16[2,2048,128]{2,1,0:T(8,128)(2,1)} %bitcast.5, f32[4,128]{1,0:T(4,128)} %bitcast.7, f32[2,16,128]{2,1,0:T(8,128)} %bitcast.6), custom_call_target="tpu_custom_call" | custom-call | tf_op jit(solution)/shard_map/pallas_call | solution.py:343
  53.8 0.6 %shard_map.60 = (f32[16,512]{1,0:T(8,128)}, f32[2,16,128]{2,1,0:T(8,128)}) custom-call(f32[16,512]{1,0:T(8,128)S(1)} %get-tuple-element.6.map_in, f32[2,16,128]{2,1,0:T(8,128)S(1)} %get-tuple-element.7.pot_in), custom_call_target="tpu_custom_call" | custom-call | tf_op jit(solution)/shard_map/pallas_call | solution.py:397

commit v8 on v6

--- a/solution.py
+++ b/solution.py
@@ -19,7 +19,7 @@
 TILES = HALF // LANES
 TGT = 8
 SLIVER = EMBED // TGT
-SPAN = 256
+SPAN = 128
 LIMIT = 40 * 1024
 MESH = pl.DeviceIdType.MESH
 F32 = jnp.float32

time: 55 us -> 54.7 us (level)
  no operation moved by 1% of the time
where the time goes in v8:
time: 54.7 us; the launch traced here: 54.6 us
  Pallas kernels  54 us (99%)
  between operations  0.64 us (1%)
    pallas_call x1, Pallas kernels, on_device(): pl.pallas_call(functools.partial(kernel, float(source_count)), out_shape=...  53.3 us

profile of v8, /device:TPU:1, one launch (start us, length us, event | category | flops | bytes accessed | tf_op | source)
XLA Modules:
  0.0 54.6 jit_solution(9676608177426105389)
XLA Ops:
  0.6 53.3 %shard_map.59 = (f32[16,512]{1,0:T(8,128)S(1)}, f32[2,16,128]{2,1,0:T(8,128)S(1)}) custom-call(bf16[512,128]{1,0:T(8,128)(2,1)} %s_hbm.1, bf16[2,2048,128]{2,1,0:T(8,128)(2,1)} %bitcast.5, f32[4,128]{1,0:T(4,128)} %bitcast.7, f32[2,16,128]{2,1,0:T(8,128)} %bitcast.6), custom_call_target="tpu_custom_call" | custom-call | tf_op jit(solution)/shard_map/pallas_call | solution.py:343
  54.0 0.6 %shard_map.60 = (f32[16,512]{1,0:T(8,128)}, f32[2,16,128]{2,1,0:T(8,128)}) custom-call(f32[16,512]{1,0:T(8,128)S(1)} %get-tuple-element.6.map_in, f32[2,16,128]{2,1,0:T(8,128)S(1)} %get-tuple-element.7.pot_in), custom_call_target="tpu_custom_call" | custom-call | tf_op jit(solution)/shard_map/pallas_call | solution.py:397
